TPU v7x, 32 devices: a whole 2x2x4 slice. The times are simulated.
32 devices in a mesh: parts: 2 (over y), latent: 16 (over z, x, core).
Axes of the slice: x: 2, y: 2, z: 4, core: 2. Of those that a mesh axis runs over, the one named last changes fastest.
Arguments:
- residual: bfloat16 [512, 4608], P(('parts', 'latent')), parts along dimension 0, may hold values from -6 to 6
- enc_weight: bfloat16 [4608, 8192], P(None, 'latent'), may hold values from -0.09375 to 0.09375
- enc_bias: float32 [8192], P('latent'), may hold values from -3 to 3
- threshold: float32 [8192], P('latent'), may hold values from 0.3 to 2
- dec_weight: bfloat16 [8192, 4608], P('latent'), may hold values from -0.1875 to 0.1875
- dec_bias: float32 [4608], replicated, may hold values from -3 to 3
- pre_gain: float32 [4608], replicated, may hold values from 0.1 to 1.9
- gate_weight: bfloat16 [4608, 2304], P(None, 'latent'), may hold values from -0.09375 to 0.09375
- up_weight: bfloat16 [4608, 2304], P(None, 'latent'), may hold values from -0.09375 to 0.09375
- down_weight: bfloat16 [2304, 4608], P('latent'), may hold values from -0.125 to 0.125
- post_gain: float32 [4608], replicated, may hold values from 0.1 to 1.9
Outputs:
- spliced_out: bfloat16 [512, 4608], P(('parts', 'latent')), parts along dimension 0
There are 2 independent parts, one for each index of `parts`. A program takes and returns all parts, laid end to end along the dimension named above; an argument that names none is the same for every part. Nothing has to cross between parts.
All inputs are finite; a program needn't handle non-finite values.
Results may differ from a plain program's by a relative error of at most 0.0057.
Values may be sent and summed in bfloat16 or wider, within the bound.
A program may use at most 128 MiB of HBM per device.

v0:
```python
import jax
import jax.numpy as jnp
from jax import lax
from jax.sharding import PartitionSpec as P

sharpness = 10.0
epsilon = 1e-06


def rms_scale(values, gain):
    return values * lax.rsqrt(jnp.mean(values * values, axis=-1, keepdims=True) + epsilon) * gain


def per_device(
    residual,
    enc_weight,
    enc_bias,
    threshold,
    dec_weight,
    dec_bias,
    pre_gain,
    gate_weight,
    up_weight,
    down_weight,
    post_gain,
):

    def encode(block_rows):
        preact = jnp.dot(block_rows, enc_weight, preferred_element_type=jnp.float32) + enc_bias
        return (preact * jax.nn.sigmoid(sharpness * (preact - threshold))).astype(jnp.bfloat16)

    def feed_hidden(block_rows):
        gate_proj = jnp.dot(block_rows, gate_weight, preferred_element_type=jnp.float32)
        up_proj = jnp.dot(block_rows, up_weight, preferred_element_type=jnp.float32)
        return (jax.nn.gelu(gate_proj, approximate=True) * up_proj).astype(jnp.bfloat16)

    def splice(local_rows):
        latent_acts = encode(lax.all_gather(local_rows, "latent", axis=0, tiled=True))
        chosen = latent_acts
        rebuilt = (
            lax.psum_scatter(
                jnp.dot(chosen, dec_weight, preferred_element_type=jnp.float32),
                "latent",
                scatter_dimension=0,
                tiled=True,
            )
            + dec_bias
        )
        normed = rms_scale(rebuilt, pre_gain).astype(jnp.bfloat16)
        hidden = feed_hidden(lax.all_gather(normed, "latent", axis=0, tiled=True))
        chosen = hidden
        ffn_sum = lax.psum_scatter(
            jnp.dot(chosen, down_weight, preferred_element_type=jnp.float32),
            "latent",
            scatter_dimension=0,
            tiled=True,
        )
        return (rebuilt + rms_scale(ffn_sum, post_gain)).astype(jnp.bfloat16)

    portions = [residual]
    results = [splice(portion) for portion in portions]
    return results[0]


def solution(mesh):
    return jax.shard_map(
        per_device,
        mesh=mesh,
        in_specs=(
            P(("parts", "latent"), None),
            P(None, "latent"),
            P("latent"),
            P("latent"),
            P("latent", None),
            P(),
            P(),
            P(None, "latent"),
            P(None, "latent"),
            P("latent", None),
            P(),
        ),
        out_specs=P(("parts", "latent"), None),
        check_vma=False,
    )
```

profile of v0, /device:TPU:0, one launch (start us, length us, event | category | flops | bytes accessed | tf_op | source)
XLA Modules:
  0.0 276.5 jit_solution(1392521232975287917)
XLA Ops:
  6.5 0.0 copy-start
  6.5 0.0 all-gather.3.cloned.1.call-start
  6.5 0.7 all-gather.3.cloned.1.call-update
  7.3 0.0 reduce-scatter.3.cloned.1.call-start
  7.3 47.4 %all-gather.3.cloned.1.call-done = bf16[256,4608]{1,0:T(8,128)(2,1)} async-done(((bf16[16,4608]{1,0:T(8,128)(2,1)}), bf16[256,4608]{1,0:T(8,128)(2,1)}) %all-gather.3.cloned.1.call-update) | async-done | bytes 2359312 | tf_op jit(solution)/shard_map/all_gather | solution.py:38
  54.7 9.4 %fusion.2 = f32[256,4608]{1,0:T(8,128)} fusion(bf16[512,4608]{1,0:T(8,128)(2,1)} %param.15, bf16[256,4608]{1,0:T(8,128)(2,1)} %all-gather.3.cloned.1.call-done, bf16[4608,512]{1,0:T(8,128)(2,1)} %param.12, f32[512]{0:T(512)} %param.14, f32[512]{0:T(512)} %param.13), kind=kOutput, calls=%fused_computation.5 | convolution fusion | flops 2416967680 | bytes 16519168 | tf_op jit(solution)/shard_map/dot_general | solution.py:42
  64.1 0.0 copy-start.3
  64.1 0.0 copy-start.4
  64.1 0.0 reduce-scatter.3.cloned.1.call-update
  64.1 0.0 copy-start.2
  64.1 0.0 all-gather.5.cloned.1.call-start
  64.1 74.4 %reduce-scatter.3.cloned.1.call-done = f32[16,4608]{1,0:T(8,128)} async-done(((f32[256,4608]{1,0:T(8,128)}), f32[16,4608]{1,0:T(8,128)}) %reduce-scatter.3.cloned.1.call-update) | async-done | bytes 294928 | tf_op jit(solution)/shard_map/reduce_scatter | solution.py:41
  138.6 0.0 copy-done.3
  138.6 1.1 multiply_reduce_fusion.1
  139.7 0.0 copy-done.4
  139.7 1.7 multiply_convert_fusion.1
  141.4 0.0 all-gather.5.cloned.1.call-update
  141.5 0.0 reduce-scatter.5.cloned.1.call-start
  141.5 41.4 %all-gather.5.cloned.1.call-done = bf16[256,4608]{1,0:T(8,128)(2,1)} async-done(((bf16[16,4608]{1,0:T(8,128)(2,1)}), bf16[256,4608]{1,0:T(8,128)(2,1)}) %all-gather.5.cloned.1.call-update) | async-done | bytes 2359312 | tf_op jit(solution)/shard_map/all_gather | solution.py:50
  183.0 2.9 %fusion.25 = f32[256,144]{0,1:T(8,128)S(1)} fusion(bf16[256,4608]{1,0:T(8,128)(2,1)} %all-gather.5.cloned.1.call-done, bf16[4608,144]{0,1:T(8,128)(2,1)} %param.18), kind=kOutput, calls=%fused_computation.34 | convolution fusion | flops 339738624 | bytes 3833856 | tf_op jit(solution)/shard_map/dot_general | solution.py:33
  185.9 0.0 copy-done
  185.9 0.0 copy-done.2
  185.9 6.6 %fusion.1 = f32[256,4608]{1,0:T(8,128)} fusion(bf16[144,4608]{1,0:T(8,128)(2,1)S(1)} %copy-done, bf16[256,4608]{1,0:T(8,128)(2,1)} %all-gather.5.cloned.1.call-done, bf16[4608,144]{0,1:T(8,128)(2,1)S(1)} %copy-done.2, f32[256,144]{0,1:T(8,128)S(1)} %fusion.25), kind=kOutput, calls=%fused_computation.3 | convolution fusion | flops 679845888 | bytes 9879552 | tf_op jit(solution)/shard_map/dot_general | solution.py:53
  192.5 0.0 copy-start.1
  192.5 0.0 copy-start.5
  192.5 0.0 reduce-scatter.5.cloned.1.call-update
  192.6 74.5 %reduce-scatter.5.cloned.1.call-done = f32[16,4608]{1,0:T(8,128)} async-done(((f32[256,4608]{1,0:T(8,128)}), f32[16,4608]{1,0:T(8,128)}) %reduce-scatter.5.cloned.1.call-update) | async-done | bytes 294928 | tf_op jit(solution)/shard_map/reduce_scatter | solution.py:52
  267.1 1.1 multiply_reduce_fusion
  268.2 0.0 copy-done.1
  268.2 0.0 copy-done.5
  268.2 1.7 add_convert_fusion
  (2 shorter events, 0.0 us)
Async XLA Ops:
  6.5 179.4 %copy-start = (bf16[144,4608]{1,0:T(8,128)(2,1)S(1)}, bf16[144,4608]{1,0:T(8,128)(2,1)}, u32[]{:S(2)}) copy-start(bf16[144,4608]{1,0:T(8,128)(2,1)} %param.20) | copy-start | bytes 3981316
  6.5 48.2 %all-gather.3.cloned.1.call-start = ((), (), s32[]{:S(2)}) async-start(), calls=%async_computation.2 | async-start | bytes 2506752 | tf_op jit(solution)/shard_map/all_gather | solution.py:38
  7.3 131.3 %reduce-scatter.3.cloned.1.call-start = ((), (), s32[]{:S(2)}) async-start(), calls=%async_computation.3 | async-start | bytes 5013504 | tf_op jit(solution)/shard_map/reduce_scatter | solution.py:41
  64.1 74.5 %copy-start.3 = (f32[4608]{0:T(1024)S(1)}, f32[4608]{0:T(1024)}, u32[]{:S(2)}) copy-start(f32[4608]{0:T(1024)} %param.16) | copy-start | bytes 55300
  64.1 75.7 %copy-start.4 = (f32[4608]{0:T(1024)S(1)}, f32[4608]{0:T(1024)}, u32[]{:S(2)}) copy-start(f32[4608]{0:T(1024)} %param.17) | copy-start | bytes 55300
  64.1 121.8 %copy-start.2 = (bf16[4608,144]{0,1:T(8,128)(2,1)S(1)}, bf16[4608,144]{0,1:T(8,128)(2,1)}, u32[]{:S(2)}) copy-start(bf16[4608,144]{0,1:T(8,128)(2,1)} %param.19) | copy-start | bytes 3981316
  64.1 118.9 %all-gather.5.cloned.1.call-start = ((), (), s32[]{:S(2)}) async-start(), calls=%async_computation.4 | async-start | bytes 2506752 | tf_op jit(solution)/shard_map/all_gather | solution.py:50
  141.5 125.6 %reduce-scatter.5.cloned.1.call-start = ((), (), s32[]{:S(2)}) async-start(), calls=%async_computation.5 | async-start | bytes 5013504 | tf_op jit(solution)/shard_map/reduce_scatter | solution.py:52
  192.5 75.7 %copy-start.1 = (f32[16,4608]{1,0:T(8,128)S(1)}, f32[16,4608]{1,0:T(8,128)}, u32[]{:S(2)}) copy-start(f32[16,4608]{1,0:T(8,128)} %reduce-scatter.3.cloned.1.call-done) | copy-start | bytes 884740
  192.5 75.7 %copy-start.5 = (f32[4608]{0:T(1024)S(1)}, f32[4608]{0:T(1024)}, u32[]{:S(2)}) copy-start(f32[4608]{0:T(1024)} %param.21) | copy-start | bytes 55300
Sparse Core Ops, SparseCore 0:
  9.6 45.0 all-gather.2
  64.2 74.3 reduce-scatter.2
  141.6 41.3 all-gather.4
  192.7 74.3 reduce-scatter.4
where the time goes:
time: 277 us; the launch traced here: 276 us
  waiting for transfers between devices  239 us (86%)
  matrix products  18.9 us (7%)
  between operations  13.2 us (5%)
  other arithmetic  5.68 us (2%)
    reduce_scatter x1, waiting for transfers between devices, splice(): lax.psum_scatter(jnp.dot(chosen, down_weight, preferred_element_type=jnp....  74.5 us
    reduce_scatter x1, waiting for transfers between devices, splice(): lax.psum_scatter(jnp.dot(chosen, dec_weight, preferred_element_type=jnp.f...  74.4 us
    all_gather x1, waiting for transfers between devices, splice(): lax.all_gather(local_rows, 'latent', axis=0, tiled=True)  47.4 us
    all_gather x1, waiting for transfers between devices, splice(): hidden = feed_hidden(lax.all_gather(normed, 'latent', axis=0, tiled=True))  41.4 us
    dot_general x1, matrix products, splice(): jnp.dot(chosen, dec_weight, preferred_element_type=jnp.float32)  9.36 us
    dot_general x1, matrix products, splice(): jnp.dot(chosen, down_weight, preferred_element_type=jnp.float32)  6.61 us
  transfers between devices with their start and end apart: 4, of which 4 were waited for; matrix products, arithmetic and copies ran while one was open for 0% of the time, Pallas kernels for 0%

commit v1 on v0

v1 whole, which is shorter than its diff:
```python
import functools

import jax
import jax.numpy as jnp
from jax import lax
from jax.experimental import pallas as pl
from jax.experimental.pallas import tpu as pltpu
from jax.sharding import PartitionSpec as P

sharpness = 10.0
epsilon = 1e-06
MESH = pl.DeviceIdType.MESH
f32 = jnp.float32
bf16 = jnp.bfloat16


def rms_scale(values, gain):
    return values * lax.rsqrt(jnp.mean(values * values, axis=-1, keepdims=True) + epsilon) * gain


def plain_device(
    residual,
    enc_weight,
    enc_bias,
    threshold,
    dec_weight,
    dec_bias,
    pre_gain,
    gate_weight,
    up_weight,
    down_weight,
    post_gain,
):
    def encode(block_rows):
        preact = jnp.dot(block_rows, enc_weight, preferred_element_type=f32) + enc_bias
        return (preact * jax.nn.sigmoid(sharpness * (preact - threshold))).astype(bf16)

    def feed_hidden(block_rows):
        gate_proj = jnp.dot(block_rows, gate_weight, preferred_element_type=f32)
        up_proj = jnp.dot(block_rows, up_weight, preferred_element_type=f32)
        return (jax.nn.gelu(gate_proj, approximate=True) * up_proj).astype(bf16)

    def scatter_sum(lhs, rhs):
        return lax.psum_scatter(
            jnp.dot(lhs, rhs, preferred_element_type=f32), "latent", scatter_dimension=0, tiled=True
        )

    latent_acts = encode(lax.all_gather(residual, "latent", axis=0, tiled=True))
    rebuilt = scatter_sum(latent_acts, dec_weight) + dec_bias
    normed = rms_scale(rebuilt, pre_gain).astype(bf16)
    hidden = feed_hidden(lax.all_gather(normed, "latent", axis=0, tiled=True))
    ffn_sum = scatter_sum(hidden, down_weight)
    return (rebuilt + rms_scale(ffn_sum, post_gain)).astype(bf16)


def chunk_of(extent):
    for pieces in (6, 4, 8, 2):
        if extent % (128 * pieces) == 0:
            return extent // pieces
    return extent


def kernel(
    Z,
    rows,
    res_ref,
    enc_hbm,
    bias_ref,
    thr_ref,
    dec_hbm,
    dec_bias_ref,
    pre_gain_ref,
    gate_hbm,
    up_hbm,
    down_hbm,
    post_gain_ref,
    out_ref,
    enc_w,
    dec_w,
    gate_w,
    up_w,
    down_w,
    gath1,
    gath2,
    own_part,
    sib_send1,
    sib_send2,
    sib_recv1,
    sib_recv2,
    x_send1,
    x_send2,
    x_recv1,
    x_recv2,
    z_send1,
    z_send2,
    up_recv1,
    up_recv2,
    dn_recv1,
    dn_recv2,
    kept,
    rebuilt_ref,
    w_sem,
    g_recv1,
    g_recv2,
    g_send1,
    g_send2,
    r_recv1,
    r_recv2,
    r_send1,
    r_send2,
):
    me = lax.axis_index("latent")
    z = me // 4
    x = (me // 2) % 2
    c = me % 2
    D = res_ref.shape[1]
    wide = chunk_of(D)
    plane = 4 * rows

    def place(pz, px, pc):
        return pz * 4 + px * 2 + pc

    def block(ref, index):
        return ref.at[pl.ds(pl.multiple_of(index * rows, rows), rows)]

    weights = [
        pltpu.make_async_copy(src, dst, w_sem.at[i])
        for i, (src, dst) in enumerate(
            [(enc_hbm, enc_w), (dec_hbm, dec_w), (gate_hbm, gate_w), (up_hbm, up_w), (down_hbm, down_w)]
        )
    ]
    for copy in weights:
        copy.start()

    has_up = z < Z - 1
    has_dn = z > 0
    barrier = pltpu.get_barrier_semaphore()

    def greet(index):
        pl.semaphore_signal(barrier, inc=1, device_id={"latent": index}, device_id_type=MESH)

    greet(place(z, x, 1 - c))
    greet(place(z, 1 - x, c))

    @pl.when(has_up)
    def _():
        greet(place(z + 1, x, c))

    @pl.when(has_dn)
    def _():
        greet(place(z - 1, x, c))

    pl.semaphore_wait(barrier, 2 + (z + Z - 1) // Z + (2 * Z - 2 - z) // Z)

    def send(src, dst, send_sem, recv_sem, index):
        return pltpu.make_async_remote_copy(
            src_ref=src,
            dst_ref=dst,
            send_sem=send_sem,
            recv_sem=recv_sem,
            device_id={"latent": index},
            device_id_type=MESH,
        )

    class Gather:
        def __init__(self, buf, send_sems, recv_sems):
            self.buf, self.send_sems, self.recv_sems = buf, send_sems, recv_sems

        def copy(self, index, slot, target):
            ref = block(self.buf, index)
            return send(ref, ref, self.send_sems.at[slot], self.recv_sems.at[index], target)

        def to_x(self, p):
            return self.copy(place(p, x, c), p, place(z, 1 - x, c))

        def to_up(self, p):
            return self.copy(place(p, x, c), Z + p, place(z + 1, x, c))

        def to_dn(self, p):
            return self.copy(place(p, x, c), 2 * Z + p, place(z - 1, x, c))

        def to_sib(self, p, px):
            return self.copy(place(p, px, c), 3 * Z + 2 * p + px, place(z, x, 1 - c))

        def await_block(self, index):
            self.copy(index, 0, place(z, x, 1 - c)).wait_recv()

        def run(self, compute):
            self.to_x(z).start()

            @pl.when(has_up)
            def _():
                self.to_up(z).start()

            @pl.when(has_dn)
            def _():
                self.to_dn(z).start()

            self.to_sib(z, x).start()

            @pl.loop(0, Z + 1)
            def _(d):
                below = z - d
                above = z + d

                @pl.when((d > 0) & (below >= 0))
                def _():
                    self.await_block(place(below, x, c))
                    self.to_x(below).start()

                    @pl.when(has_up)
                    def _():
                        self.to_up(below).start()

                    self.to_sib(below, x).start()

                @pl.when((d > 0) & (above < Z))
                def _():
                    self.await_block(place(above, x, c))
                    self.to_x(above).start()

                    @pl.when(has_dn)
                    def _():
                        self.to_dn(above).start()

                    self.to_sib(above, x).start()

                @pl.loop(0, 2)
                def _(side):
                    p = z + (2 * side - 1) * (d - 1)

                    @pl.when((d > 0) & (p >= 0) & (p < Z) & (d + 1 - side > 1))
                    def _():
                        self.await_block(place(p, 1 - x, c))
                        self.to_sib(p, 1 - x).start()
                        self.await_block(place(p, x, 1 - c))
                        self.await_block(place(p, 1 - x, 1 - c))
                        compute(p)

        def drain(self):
            for p in range(Z):
                self.to_x(p).wait_send()
                self.to_sib(p, 0).wait_send()
                self.to_sib(p, 1).wait_send()

                @pl.when(has_up & (p <= z))
                def _():
                    self.to_up(p).wait_send()

                @pl.when(has_dn & (p >= z))
                def _():
                    self.to_dn(p).wait_send()

    class Scatter:
        def __init__(self, sib_send, sib_recv, x_send, x_recv, z_send, up_recv, dn_recv, send_sems, recv_sems):
            self.sib_send, self.sib_recv = sib_send, sib_recv
            self.x_send, self.x_recv = x_send, x_recv
            self.z_send, self.up_recv, self.dn_recv = z_send, up_recv, dn_recv
            self.send_sems, self.recv_sems = send_sems, recv_sems

        def copy(self, src, dst, kind, p, target):
            return send(src.at[p], dst.at[p], self.send_sems.at[kind * Z + p], self.recv_sems.at[kind * Z + p], target)

        def to_sib(self, p):
            return self.copy(self.sib_send, self.sib_recv, 0, p, place(z, x, 1 - c))

        def to_x(self, p):
            return self.copy(self.x_send, self.x_recv, 1, p, place(z, 1 - x, c))

        def to_up(self, p):
            return self.copy(self.z_send, self.up_recv, 2, p, place(z + 1, x, c))

        def to_dn(self, p):
            return self.copy(self.z_send, self.dn_recv, 3, p, place(z - 1, x, c))

        def project(self, p, acts, weight):
            blocks = [acts[i * rows : (i + 1) * rows] for i in range(4)]
            first = c == 0
            lhs = jnp.concatenate(
                [
                    jnp.where(first, blocks[1], blocks[0]),
                    jnp.where(first, blocks[3], blocks[2]),
                    jnp.where(first, blocks[0], blocks[1]),
                    jnp.where(first, blocks[2], blocks[3]),
                ],
                axis=0,
            ).astype(bf16)

            @pl.loop(0, D // wide)
            def _(k):
                cols = pl.ds(pl.multiple_of(k * wide, wide), wide)
                term = jnp.dot(lhs, weight[:, cols], preferred_element_type=f32)
                for i in range(2):
                    self.sib_send[p, i, :, cols] = term[i * rows : (i + 1) * rows].astype(bf16)
                    own_part[p, i, :, cols] = term[(2 + i) * rows : (3 + i) * rows]

            self.to_sib(p).start()

        def run(self):
            @pl.loop(0, 2 * Z)
            def _(i):
                d = Z - 1 - i // 2
                p = z + (2 * (i % 2) - 1) * d

                @pl.when((p >= 0) & (p < Z) & (d + 1 - i % 2 > 0))
                def _():
                    self.to_sib(p).wait_recv()
                    self.x_send[p] = (
                        own_part[p, 1 - x] + self.sib_recv[p, 1 - x].astype(f32)
                    ).astype(bf16)
                    self.to_x(p).start()
                    kept[p] = own_part[p, x] + self.sib_recv[p, x].astype(f32)

            @pl.loop(0, 2 * Z - 2)
            def _(i):
                d = Z - 1 - i // 2
                p = z + (2 * (i % 2) - 1) * d

                @pl.when((p >= 0) & (p < z))
                def _():
                    self.to_x(p).wait_recv()

                    @pl.when(has_up)
                    def _():
                        self.to_dn(p).wait_recv()
                        self.z_send[p] = (
                            kept[p] + self.x_recv[p].astype(f32) + self.dn_recv[p].astype(f32)
                        ).astype(bf16)

                    @pl.when(z == Z - 1)
                    def _():
                        self.z_send[p] = (kept[p] + self.x_recv[p].astype(f32)).astype(bf16)

                    self.to_dn(p).start()

                @pl.when((p > z) & (p < Z))
                def _():
                    self.to_x(p).wait_recv()

                    @pl.when(has_dn)
                    def _():
                        self.to_up(p).wait_recv()
                        self.z_send[p] = (
                            kept[p] + self.x_recv[p].astype(f32) + self.up_recv[p].astype(f32)
                        ).astype(bf16)

                    @pl.when(z == 0)
                    def _():
                        self.z_send[p] = (kept[p] + self.x_recv[p].astype(f32)).astype(bf16)

                    self.to_up(p).start()

            self.to_x(z).wait_recv()
            kept[z] += self.x_recv[z].astype(f32)

            @pl.when(has_up)
            def _():
                self.to_dn(z).wait_recv()
                kept[z] += self.dn_recv[z].astype(f32)

            @pl.when(has_dn)
            def _():
                self.to_up(z).wait_recv()
                kept[z] += self.up_recv[z].astype(f32)

            return kept[z]

        def drain(self):
            for p in range(Z):
                self.to_sib(p).wait_send()
                self.to_x(p).wait_send()

                @pl.when(p > z)
                def _():
                    self.to_up(p).wait_send()

                @pl.when(p < z)
                def _():
                    self.to_dn(p).wait_send()

    gather1 = Gather(gath1, g_send1, g_recv1)
    gather2 = Gather(gath2, g_send2, g_recv2)
    scatter1 = Scatter(
        sib_send1, sib_recv1, x_send1, x_recv1, z_send1, up_recv1, dn_recv1, r_send1, r_recv1
    )
    scatter2 = Scatter(
        sib_send2, sib_recv2, x_send2, x_recv2, z_send2, up_recv2, dn_recv2, r_send2, r_recv2
    )

    def product(buf, p, mats):
        lhs_rows = pl.ds(pl.multiple_of(p * plane, plane), plane)

        def step(k, sums):
            part = pl.ds(pl.multiple_of(k * wide, wide), wide)
            lhs = buf[lhs_rows, part]
            return tuple(
                total + jnp.dot(lhs, mat[part, :], preferred_element_type=f32)
                for total, mat in zip(sums, mats)
            )

        zeros = tuple(jnp.zeros((plane, mat.shape[1]), f32) for mat in mats)
        return lax.fori_loop(0, D // wide, step, zeros)

    def encode(p):
        (total,) = product(gath1, p, (enc_w,))
        preact = total + bias_ref[...]
        acts = preact * jax.nn.sigmoid(sharpness * (preact - thr_ref[...]))
        scatter1.project(p, acts, dec_w)

    def feed_hidden(p):
        gate_proj, up_proj = product(gath2, p, (gate_w, up_w))
        scatter2.project(p, jax.nn.gelu(gate_proj, approximate=True) * up_proj, down_w)

    block(gath1, me)[...] = res_ref[...]
    weights[0].wait()
    weights[1].wait()
    gather1.run(encode)
    rebuilt = scatter1.run() + dec_bias_ref[...]
    rebuilt_ref[...] = rebuilt
    block(gath2, me)[...] = rms_scale(rebuilt, pre_gain_ref[...]).astype(bf16)
    weights[2].wait()
    weights[3].wait()
    weights[4].wait()
    gather2.run(feed_hidden)
    ffn_sum = scatter2.run()
    out_ref[...] = (rebuilt_ref[...] + rms_scale(ffn_sum, post_gain_ref[...])).astype(bf16)
    for phase in (gather1, scatter1, gather2, scatter2):
        phase.drain()


def fused_device(
    n,
    residual,
    enc_weight,
    enc_bias,
    threshold,
    dec_weight,
    dec_bias,
    pre_gain,
    gate_weight,
    up_weight,
    down_weight,
    post_gain,
):
    rows, D = residual.shape
    Z = n // 4
    vmem = pl.BlockSpec(memory_space=pltpu.VMEM)
    hbm = pl.BlockSpec(memory_space=pl.ANY)

    def twice(shape, dtype):
        return [pltpu.VMEM(shape, dtype)] * 2

    def sems(count):
        return [pltpu.SemaphoreType.DMA((count,))] * 2

    latents, hidden = enc_weight.shape[1], gate_weight.shape[1]
    return pl.pallas_call(
        functools.partial(kernel, Z, rows),
        out_shape=jax.ShapeDtypeStruct(residual.shape, bf16),
        in_specs=[vmem, hbm, vmem, vmem, hbm, vmem, vmem, hbm, hbm, hbm, vmem],
        out_specs=vmem,
        scratch_shapes=[
            pltpu.VMEM(enc_weight.shape, bf16),
            pltpu.VMEM(dec_weight.shape, bf16),
            pltpu.VMEM(gate_weight.shape, bf16),
            pltpu.VMEM(up_weight.shape, bf16),
            pltpu.VMEM(down_weight.shape, bf16),
            *twice((n * rows, D), bf16),
            pltpu.VMEM((Z, 2, rows, D), f32),
            *twice((Z, 2, rows, D), bf16),
            *twice((Z, 2, rows, D), bf16),
            *twice((Z, rows, D), bf16),
            *twice((Z, rows, D), bf16),
            *twice((Z, rows, D), bf16),
            *twice((Z, rows, D), bf16),
            *twice((Z, rows, D), bf16),
            pltpu.VMEM((Z, rows, D), f32),
            pltpu.VMEM((rows, D), f32),
            pltpu.SemaphoreType.DMA((5,)),
            *sems(n),
            *sems(5 * Z),
            *sems(4 * Z),
            *sems(4 * Z),
        ],
        compiler_params=pltpu.CompilerParams(
            collective_id=0, has_side_effects=True, vmem_limit_bytes=52 * 1024 * 1024
        ),
        cost_estimate=pl.CostEstimate(
            flops=2 * n * rows * D * (2 * latents + 3 * hidden),
            bytes_accessed=2 * D * (2 * latents + 3 * hidden),
            transcendentals=n * rows * (latents + hidden),
        ),
    )(
        residual,
        enc_weight,
        enc_bias.reshape(1, -1),
        threshold.reshape(1, -1),
        dec_weight,
        dec_bias.reshape(1, -1),
        pre_gain.reshape(1, -1),
        gate_weight,
        up_weight,
        down_weight,
        post_gain.reshape(1, -1),
    )


def solution(mesh):
    n = mesh.shape["latent"]

    def per_device(residual, *rest):
        rows, width = residual.shape
        if n % 4 == 0 and rows % 16 == 0 and width % 128 == 0:
            return fused_device(n, residual, *rest)
        return plain_device(residual, *rest)

    return jax.shard_map(
        per_device,
        mesh=mesh,
        in_specs=(
            P(("parts", "latent"), None),
            P(None, "latent"),
            P("latent"),
            P("latent"),
            P("latent", None),
            P(),
            P(),
            P(None, "latent"),
            P(None, "latent"),
            P("latent", None),
            P(),
        ),
        out_specs=P(("parts", "latent"), None),
        check_vma=False,
    )
```

time: 277 us -> 106 us (0.38)
  waiting for transfers between devices: 239 us -> 0 us
  Pallas kernels: 0 us -> 96 us
  matrix products: 18.9 us -> 0 us
  between operations: 13.2 us -> 0.05 us
  local copies, waits for them, and re-layouts: 0.03 us -> 9.22 us
  other arithmetic: 5.68 us -> 0 us
    reduce_scatter x2 -> x0, waiting for transfers between devices: 149 us -> none  [the longest x1 74.5 us: splice(): lax.psum_scatter(jnp.dot(chosen, down_weight, preferred_element_type=jnp....]
    pallas_call x0 -> x1, Pallas kernels: none -> 96 us  [fused_device(): pl.pallas_call(functools.partial(kernel, Z, rows), out_shape=jax.ShapeDty...]
    all_gather x2 -> x0, waiting for transfers between devices: 88.8 us -> none  [the longest x1 47.4 us: splice(): lax.all_gather(local_rows, 'latent', axis=0, tiled=True)]
    dot_general x3 -> x0, matrix products: 18.9 us -> none  [the longest x1 9.36 us: splice(): jnp.dot(chosen, dec_weight, preferred_element_type=jnp.float32)]
    unnamed x12 -> x13, local copies, waits for them, and re-layouts: 0.03 us -> 6.89 us
    convert_element_type x2 -> x0, other arithmetic: 3.45 us -> none  [the longest x1 1.73 us: splice(): return (rebuilt + rms_scale(ffn_sum, post_gain)).astype(jnp.bfloat16)]
  transfers between devices with their start and end apart: 4 -> 0, of which waited for: 4 -> 0; matrix products, arithmetic and copies ran while one was open for 0% -> 0% of each run, Pallas kernels for 0% -> 0%
where the time goes in v1:
time: 106 us; the launch traced here: 105 us
  Pallas kernels  96 us (91%)
  local copies, waits for them, and re-layouts  9.22 us (9%)
    pallas_call x1, Pallas kernels, fused_device(): pl.pallas_call(functools.partial(kernel, Z, rows), out_shape=jax.ShapeDty...  96 us
    unnamed x13, local copies, waits for them, and re-layouts  6.89 us

profile of v1, /device:TPU:0, one launch (start us, length us, event | category | flops | bytes accessed | tf_op | source)
XLA Modules:
  0.0 105.3 jit_solution(4322729907948082501)
XLA Ops:
  0.0 0.0 copy-start.4
  0.0 0.8 reshape.17.dec_bias_ref
  0.9 0.7 reshape.18.pre_gain_ref
  1.6 0.7 reshape.19.post_gain_ref
  2.3 3.8 %copy.12.gate_hbm = bf16[4608,144]{1,0:T(8,128)(2,1)} copy(bf16[4608,144]{0,1:T(8,128)(2,1)} %param.18) | data formatting | bytes 2654208 | tf_op args[7]
  6.1 0.0 copy-done.4
  6.1 0.0 copy-start
  6.1 0.0 copy-start.1
  6.1 0.0 copy-start.2
  6.2 0.0 copy-start.3
  6.2 2.4 %copy.13.up_hbm = bf16[4608,144]{1,0:T(8,128)(2,1)} copy(bf16[4608,144]{0,1:T(8,128)(2,1)S(1)} %copy-done.4) | data formatting | bytes 2654208 | tf_op args[8]
  8.6 0.0 copy-done
  8.6 0.0 copy-done.1
  8.6 0.0 copy-done.2
  8.6 0.0 copy-done.3
  8.6 96.0 %shard_map.109 = bf16[16,4608]{1,0:T(8,128)(2,1)S(1)} custom-call(bf16[16,4608]{1,0:T(8,128)(2,1)S(1)} %copy-done.1, bf16[4608,512]{1,0:T(8,128)(2,1)} %enc_hbm.1, f32[1,512]{1,0:T(1,128)S(1)} %bitcast.2, f32[1,512]{1,0:T(1,128)S(1)} %bitcast.3, bf16[512,4608]{1,0:T(8,128)(2,1)} %dec_hbm.1, f32[1,4608]{1,0:T(1,128)S(1)} %reshape.17.dec_bias_ref, ...), custom_call_target="tpu_custom_call" | custom-call | flops 3435134976 | bytes 13418496 | tf_op jit(solution)/shard_map/pallas_call | solution.py:457
  104.6 0.7 copy.15
Async XLA Ops:
  0.0 6.1 %copy-start.4 = (bf16[4608,144]{0,1:T(8,128)(2,1)S(1)}, bf16[4608,144]{0,1:T(8,128)(2,1)}, u32[]{:S(2)}) copy-start(bf16[4608,144]{0,1:T(8,128)(2,1)} %param.19) | copy-start | bytes 3981316
  6.1 2.4 %copy-start = (bf16[144,4608]{1,0:T(8,128)(2,1)S(1)}, bf16[144,4608]{1,0:T(8,128)(2,1)}, u32[]{:S(2)}) copy-start(bf16[144,4608]{1,0:T(8,128)(2,1)} %down_hbm.1) | copy-start | bytes 3981316
  6.1 2.4 %copy-start.1 = (bf16[16,4608]{1,0:T(8,128)(2,1)S(1)}, bf16[16,4608]{1,0:T(8,128)(2,1)}, u32[]{:S(2)}) copy-start(bf16[16,4608]{1,0:T(8,128)(2,1)} %res_ref.1) | copy-start | bytes 442372
  6.1 2.4 %copy-start.2 = (f32[512]{0:T(512)S(1)}, f32[512]{0:T(512)}, u32[]{:S(2)}) copy-start(f32[512]{0:T(512)} %param.13) | copy-start | bytes 6148
  6.2 2.4 %copy-start.3 = (f32[512]{0:T(512)S(1)}, f32[512]{0:T(512)}, u32[]{:S(2)}) copy-start(f32[512]{0:T(512)} %param.14) | copy-start | bytes 6148

commit v2 on v1

--- a/solution.py
+++ b/solution.py
@@ -51,6 +51,10 @@
     hidden = feed_hidden(lax.all_gather(normed, "latent", axis=0, tiled=True))
     ffn_sum = scatter_sum(hidden, down_weight)
     return (rebuilt + rms_scale(ffn_sum, post_gain)).astype(bf16)
+
+
+def halves_of(extent):
+    return 2 if extent % 256 == 0 else 1
 
 
 def chunk_of(extent):
@@ -115,10 +119,22 @@
     c = me % 2
     D = res_ref.shape[1]
     wide = chunk_of(D)
+    halves = halves_of(D)
+    half = D // halves
     plane = 4 * rows
 
     def place(pz, px, pc):
         return pz * 4 + px * 2 + pc
+
+    arrival = [sorted(range(Z), key=lambda p: (abs(p - own), p)) for own in range(Z)]
+    leaving = [[order[-2], order[-1], *order[-3::-1]] for order in arrival]
+
+    def pick(table, k):
+        value = 0
+        for own in range(Z):
+            for place_in_order in range(Z):
+                value += jnp.where((z == own) & (k == place_in_order), table[own][place_in_order], 0)
+        return value
 
     def block(ref, index):
         return ref.at[pl.ds(pl.multiple_of(index * rows, rows), rows)]
@@ -129,8 +145,8 @@
             [(enc_hbm, enc_w), (dec_hbm, dec_w), (gate_hbm, gate_w), (up_hbm, up_w), (down_hbm, down_w)]
         )
     ]
-    for copy in weights:
-        copy.start()
+    weights[0].start()
+    weights[1].start()
 
     has_up = z < Z - 1
     has_dn = z > 0
@@ -185,7 +201,7 @@
         def await_block(self, index):
             self.copy(index, 0, place(z, x, 1 - c)).wait_recv()
 
-        def run(self, compute):
+        def run(self, compute, before_last):
             self.to_x(z).start()
 
             @pl.when(has_up)
@@ -235,6 +251,11 @@
                         self.to_sib(p, 1 - x).start()
                         self.await_block(place(p, x, 1 - c))
                         self.await_block(place(p, 1 - x, 1 - c))
+
+                        @pl.when(p == pick(arrival, Z - 1))
+                        def _():
+                            before_last()
+
                         compute(p)
 
         def drain(self):
@@ -258,20 +279,26 @@
             self.z_send, self.up_recv, self.dn_recv = z_send, up_recv, dn_recv
             self.send_sems, self.recv_sems = send_sems, recv_sems
 
-        def copy(self, src, dst, kind, p, target):
-            return send(src.at[p], dst.at[p], self.send_sems.at[kind * Z + p], self.recv_sems.at[kind * Z + p], target)
+        def copy(self, src, dst, kind, p, h, target):
+            cols = pl.ds(pl.multiple_of(h * half, half), half)
+            slot = kind * Z * halves + p * halves + h
+            return send(
+                src.at[p, :, cols], dst.at[p, :, cols], self.send_sems.at[slot], self.recv_sems.at[slot], target
+            )
 
         def to_sib(self, p):
-            return self.copy(self.sib_send, self.sib_recv, 0, p, place(z, x, 1 - c))
-
-        def to_x(self, p):
-            return self.copy(self.x_send, self.x_recv, 1, p, place(z, 1 - x, c))
-
-        def to_up(self, p):
-            return self.copy(self.z_send, self.up_recv, 2, p, place(z + 1, x, c))
-
-        def to_dn(self, p):
-            return self.copy(self.z_send, self.dn_recv, 3, p, place(z - 1, x, c))
+            return send(
+                self.sib_send.at[p], self.sib_recv.at[p], self.send_sems.at[p], self.recv_sems.at[p], place(z, x, 1 - c)
+            )
+
+        def to_x(self, p, h):
+            return self.copy(self.x_send, self.x_recv, 1, p, h, place(z, 1 - x, c))
+
+        def to_up(self, p, h):
+            return self.copy(self.z_send, self.up_recv, 2, p, h, place(z + 1, x, c))
+
+        def to_dn(self, p, h):
+            return self.copy(self.z_send, self.dn_recv, 3, p, h, place(z - 1, x, c))
 
         def project(self, p, acts, weight):
             blocks = [acts[i * rows : (i + 1) * rows] for i in range(4)]
@@ -296,87 +323,74 @@
 
             self.to_sib(p).start()
 
+        def start_x(self, j):
+            p, h = pick(leaving, j // halves), j % halves
+            cols = pl.ds(pl.multiple_of(h * half, half), half)
+
+            @pl.when(h == 0)
+            def _():
+                self.to_sib(p).wait_recv()
+
+            self.x_send[p, :, cols] = (
+                own_part[p, 1 - x, :, cols] + self.sib_recv[p, 1 - x, :, cols].astype(f32)
+            ).astype(bf16)
+            self.to_x(p, h).start()
+            kept[p, :, cols] = own_part[p, x, :, cols] + self.sib_recv[p, x, :, cols].astype(f32)
+
+        def start_first(self):
+            for j in range(halves):
+                self.start_x(j)
+
         def run(self):
-            @pl.loop(0, 2 * Z)
-            def _(i):
-                d = Z - 1 - i // 2
-                p = z + (2 * (i % 2) - 1) * d
-
-                @pl.when((p >= 0) & (p < Z) & (d + 1 - i % 2 > 0))
-                def _():
-                    self.to_sib(p).wait_recv()
-                    self.x_send[p] = (
-                        own_part[p, 1 - x] + self.sib_recv[p, 1 - x].astype(f32)
-                    ).astype(bf16)
-                    self.to_x(p).start()
-                    kept[p] = own_part[p, x] + self.sib_recv[p, x].astype(f32)
-
-            @pl.loop(0, 2 * Z - 2)
-            def _(i):
-                d = Z - 1 - i // 2
-                p = z + (2 * (i % 2) - 1) * d
-
-                @pl.when((p >= 0) & (p < z))
-                def _():
-                    self.to_x(p).wait_recv()
-
-                    @pl.when(has_up)
-                    def _():
-                        self.to_dn(p).wait_recv()
-                        self.z_send[p] = (
-                            kept[p] + self.x_recv[p].astype(f32) + self.dn_recv[p].astype(f32)
-                        ).astype(bf16)
-
-                    @pl.when(z == Z - 1)
-                    def _():
-                        self.z_send[p] = (kept[p] + self.x_recv[p].astype(f32)).astype(bf16)
-
-                    self.to_dn(p).start()
-
-                @pl.when((p > z) & (p < Z))
-                def _():
-                    self.to_x(p).wait_recv()
-
-                    @pl.when(has_dn)
-                    def _():
-                        self.to_up(p).wait_recv()
-                        self.z_send[p] = (
-                            kept[p] + self.x_recv[p].astype(f32) + self.up_recv[p].astype(f32)
-                        ).astype(bf16)
-
-                    @pl.when(z == 0)
-                    def _():
-                        self.z_send[p] = (kept[p] + self.x_recv[p].astype(f32)).astype(bf16)
-
-                    self.to_up(p).start()
-
-            self.to_x(z).wait_recv()
-            kept[z] += self.x_recv[z].astype(f32)
-
-            @pl.when(has_up)
-            def _():
-                self.to_dn(z).wait_recv()
-                kept[z] += self.dn_recv[z].astype(f32)
-
-            @pl.when(has_dn)
-            def _():
-                self.to_up(z).wait_recv()
-                kept[z] += self.up_recv[z].astype(f32)
+            @pl.loop(0, Z * halves)
+            def _(j):
+                p, h = pick(leaving, j // halves), j % halves
+                cols = pl.ds(pl.multiple_of(h * half, half), half)
+                self.to_x(p, h).wait_send()
+
+                @pl.when(j + halves < Z * halves)
+                def _():
+                    self.start_x(j + halves)
+
+                self.to_x(p, h).wait_recv()
+                kept[p, :, cols] += self.x_recv[p, :, cols].astype(f32)
+
+                @pl.when((p <= z) & has_up)
+                def _():
+                    self.to_dn(p, h).wait_recv()
+                    kept[p, :, cols] += self.dn_recv[p, :, cols].astype(f32)
+
+                @pl.when((p >= z) & has_dn)
+                def _():
+                    self.to_up(p, h).wait_recv()
+                    kept[p, :, cols] += self.up_recv[p, :, cols].astype(f32)
+
+                @pl.when(p != z)
+                def _():
+                    self.z_send[p, :, cols] = kept[p, :, cols].astype(bf16)
+
+                @pl.when(p < z)
+                def _():
+                    self.to_dn(p, h).start()
+
+                @pl.when(p > z)
+                def _():
+                    self.to_up(p, h).start()
 
             return kept[z]
 
         def drain(self):
             for p in range(Z):
                 self.to_sib(p).wait_send()
-                self.to_x(p).wait_send()
-
-                @pl.when(p > z)
-                def _():
-                    self.to_up(p).wait_send()
-
-                @pl.when(p < z)
-                def _():
-                    self.to_dn(p).wait_send()
+                for h in range(halves):
+
+                    @pl.when(p > z)
+                    def _():
+                        self.to_up(p, h).wait_send()
+
+                    @pl.when(p < z)
+                    def _():
+                        self.to_dn(p, h).wait_send()
 
     gather1 = Gather(gath1, g_send1, g_recv1)
     gather2 = Gather(gath2, g_send2, g_recv2)
@@ -387,43 +401,51 @@
         sib_send2, sib_recv2, x_send2, x_recv2, z_send2, up_recv2, dn_recv2, r_send2, r_recv2
     )
 
-    def product(buf, p, mats):
-        lhs_rows = pl.ds(pl.multiple_of(p * plane, plane), plane)
-
-        def step(k, sums):
-            part = pl.ds(pl.multiple_of(k * wide, wide), wide)
-            lhs = buf[lhs_rows, part]
+    def lhs_of(buf, p, k):
+        return buf[pl.ds(pl.multiple_of(p * plane, plane), plane), part_of(k)]
+
+    def part_of(k):
+        return pl.ds(pl.multiple_of(k * wide, wide), wide)
+
+    def encode(p):
+        @pl.when(p == z)
+        def _():
+            weights[0].wait()
+            weights[1].wait()
+            for copy in weights[2:]:
+                copy.start()
+
+        def step(k, total):
+            return total + jnp.dot(lhs_of(gath1, p, k), enc_w[part_of(k), :], preferred_element_type=f32)
+
+        total = lax.fori_loop(0, D // wide, step, jnp.zeros((plane, enc_w.shape[1]), f32))
+        preact = total + bias_ref[...].reshape(1, -1)
+        acts = preact * jax.nn.sigmoid(sharpness * (preact - thr_ref[...].reshape(1, -1)))
+        scatter1.project(p, acts, dec_w)
+
+    def feed_hidden(p):
+        def step(k, totals):
+            lhs = lhs_of(gath2, p, k)
             return tuple(
-                total + jnp.dot(lhs, mat[part, :], preferred_element_type=f32)
-                for total, mat in zip(sums, mats)
+                total
+                + lax.dot_general(lhs, mat[:, part_of(k)], (((1,), (1,)), ((), ())), preferred_element_type=f32)
+                for total, mat in zip(totals, (gate_w, up_w))
             )
 
-        zeros = tuple(jnp.zeros((plane, mat.shape[1]), f32) for mat in mats)
-        return lax.fori_loop(0, D // wide, step, zeros)
-
-    def encode(p):
-        (total,) = product(gath1, p, (enc_w,))
-        preact = total + bias_ref[...]
-        acts = preact * jax.nn.sigmoid(sharpness * (preact - thr_ref[...]))
-        scatter1.project(p, acts, dec_w)
-
-    def feed_hidden(p):
-        gate_proj, up_proj = product(gath2, p, (gate_w, up_w))
+        zeros = jnp.zeros((plane, gate_w.shape[0]), f32)
+        gate_proj, up_proj = lax.fori_loop(0, D // wide, step, (zeros, zeros))
         scatter2.project(p, jax.nn.gelu(gate_proj, approximate=True) * up_proj, down_w)
 
     block(gath1, me)[...] = res_ref[...]
-    weights[0].wait()
-    weights[1].wait()
-    gather1.run(encode)
-    rebuilt = scatter1.run() + dec_bias_ref[...]
+    gather1.run(encode, scatter1.start_first)
+    rebuilt = scatter1.run() + dec_bias_ref[...].reshape(1, -1)
     rebuilt_ref[...] = rebuilt
-    block(gath2, me)[...] = rms_scale(rebuilt, pre_gain_ref[...]).astype(bf16)
-    weights[2].wait()
-    weights[3].wait()
-    weights[4].wait()
-    gather2.run(feed_hidden)
+    block(gath2, me)[...] = rms_scale(rebuilt, pre_gain_ref[...].reshape(1, -1)).astype(bf16)
+    for copy in weights[2:]:
+        copy.wait()
+    gather2.run(feed_hidden, scatter2.start_first)
     ffn_sum = scatter2.run()
-    out_ref[...] = (rebuilt_ref[...] + rms_scale(ffn_sum, post_gain_ref[...])).astype(bf16)
+    out_ref[...] = (rebuilt_ref[...] + rms_scale(ffn_sum, post_gain_ref[...].reshape(1, -1))).astype(bf16)
     for phase in (gather1, scatter1, gather2, scatter2):
         phase.drain()
 
@@ -462,8 +484,8 @@
         scratch_shapes=[
             pltpu.VMEM(enc_weight.shape, bf16),
             pltpu.VMEM(dec_weight.shape, bf16),
-            pltpu.VMEM(gate_weight.shape, bf16),
-            pltpu.VMEM(up_weight.shape, bf16),
+            pltpu.VMEM(gate_weight.shape[::-1], bf16),
+            pltpu.VMEM(up_weight.shape[::-1], bf16),
             pltpu.VMEM(down_weight.shape, bf16),
             *twice((n * rows, D), bf16),
             pltpu.VMEM((Z, 2, rows, D), f32),
@@ -479,11 +501,11 @@
             pltpu.SemaphoreType.DMA((5,)),
             *sems(n),
             *sems(5 * Z),
-            *sems(4 * Z),
-            *sems(4 * Z),
+            *sems(4 * Z * halves_of(D)),
+            *sems(4 * Z * halves_of(D)),
         ],
         compiler_params=pltpu.CompilerParams(
-            collective_id=0, has_side_effects=True, vmem_limit_bytes=52 * 1024 * 1024
+            collective_id=0, has_side_effects=True, vmem_limit_bytes=60 * 1024 * 1024
         ),
         cost_estimate=pl.CostEstimate(
             flops=2 * n * rows * D * (2 * latents + 3 * hidden),
@@ -493,15 +515,15 @@
     )(
         residual,
         enc_weight,
-        enc_bias.reshape(1, -1),
-        threshold.reshape(1, -1),
+        enc_bias,
+        threshold,
         dec_weight,
-        dec_bias.reshape(1, -1),
-        pre_gain.reshape(1, -1),
-        gate_weight,
-        up_weight,
+        dec_bias,
+        pre_gain,
+        gate_weight.T,
+        up_weight.T,
         down_weight,
-        post_gain.reshape(1, -1),
+        post_gain,
     )
 
 

time: 106 us -> 104 us (0.981)
  local copies, waits for them, and re-layouts: 9.22 us -> 1.58 us
  Pallas kernels: 96 us -> 103 us
    pallas_call x1, Pallas kernels: 96 us -> 103 us  [fused_device(): pl.pallas_call(functools.partial(kernel, Z, rows), out_shape=jax.ShapeDty...]
    unnamed x13 -> x1, local copies, waits for them, and re-layouts: 6.89 us -> 1.58 us
    reshape x3 -> x0, local copies, waits for them, and re-layouts: 2.33 us -> none  [the longest x1 0.85 us: fused_device(): dec_bias.reshape(1, -1)]
where the time goes in v2:
time: 104 us
  Pallas kernels  103 us (99%)
  local copies, waits for them, and re-layouts  1.58 us (2%)
    pallas_call x1, Pallas kernels, fused_device(): pl.pallas_call(functools.partial(kernel, Z, rows), out_shape=jax.ShapeDty...  103 us

profile of v2, /device:TPU:0, one launch (start us, length us, event | category | flops | bytes accessed | tf_op | source)
XLA Modules:
  0.0 104.3 jit_solution(17262784647521993164)
XLA Ops:
  0.0 102.8 %shard_map.109 = bf16[16,4608]{1,0:T(8,128)(2,1)} custom-call(bf16[16,4608]{1,0:T(8,128)(2,1)} %res_ref.1, bf16[4608,512]{1,0:T(8,128)(2,1)} %enc_hbm.1, f32[512]{0:T(512)} %bias_ref.1, f32[512]{0:T(512)} %thr_ref.1, bf16[512,4608]{1,0:T(8,128)(2,1)} %dec_hbm.1, f32[4608]{0:T(1024)} %dec_bias_ref.1, f32[4608]{0:T(1024)} %pre_gain_ref.1, ...), custom_call_target="tpu_custom_call" | custom-call | flops 3435134976 | bytes 13418496 | tf_op jit(solution)/shard_map/pallas_call | solution.py:479
  102.8 1.6 %copy.13 = bf16[16,4608]{1,0:T(8,128)(2,1)} copy(bf16[16,4608]{1,0:T(8,128)(2,1)} %shard_map.109) | data formatting | bytes 294912

commit v3 on v2

--- a/solution.py
+++ b/solution.py
@@ -126,13 +126,20 @@
     def place(pz, px, pc):
         return pz * 4 + px * 2 + pc
 
-    arrival = [sorted(range(Z), key=lambda p: (abs(p - own), p)) for own in range(Z)]
-    leaving = [[order[-2], order[-1], *order[-3::-1]] for order in arrival]
+    def order_of(own):
+        step = 1 - 2 * (own % 2)
+        planes = [own] + [own + side * step * d for d in range(1, Z) for side in (1, -1)]
+        return [p for p in planes if 0 <= p < Z]
+
+    arrival = [order_of(own) for own in range(Z)]
+    leaving = [[order[1], *order[:1:-1], order[0]] for order in arrival]
+    passing = [[order[-1], order[1], *order[-2:1:-1], order[0]] for order in arrival]
+    groups = [sorted(range(Z // 2), key=lambda g: (abs(g - own // 2), g)) for own in range(Z)]
 
     def pick(table, k):
         value = 0
         for own in range(Z):
-            for place_in_order in range(Z):
+            for place_in_order in range(len(table[own])):
                 value += jnp.where((z == own) & (k == place_in_order), table[own][place_in_order], 0)
         return value
 
@@ -213,54 +220,70 @@
                 self.to_dn(z).start()
 
             self.to_sib(z, x).start()
-
-            @pl.loop(0, Z + 1)
-            def _(d):
-                below = z - d
-                above = z + d
-
-                @pl.when((d > 0) & (below >= 0))
-                def _():
-                    self.await_block(place(below, x, c))
-                    self.to_x(below).start()
-
-                    @pl.when(has_up)
+            toward = 1 - 2 * (z % 2)
+
+            for d in range(1, Z):
+                first, second = z + toward * d, z - toward * d
+                first_is = (first >= 0) & (first < Z)
+
+                @pl.when(first_is)
+                def _():
+                    self.pass_on(first)
+                    self.to_x(first).start()
+
+                @pl.when((second >= 0) & (second < Z))
+                def _():
+                    self.pass_on(second)
+
+                    @pl.when(first_is)
                     def _():
-                        self.to_up(below).start()
-
-                    self.to_sib(below, x).start()
-
-                @pl.when((d > 0) & (above < Z))
-                def _():
-                    self.await_block(place(above, x, c))
-                    self.to_x(above).start()
-
-                    @pl.when(has_dn)
+                        self.to_x(first).wait_send()
+
+                    self.to_x(second).start()
+
+            @pl.loop(0, Z // 2)
+            def _(g):
+                for k in range(Z):
+
+                    @pl.when(g == (0 if k < 2 else 1))
                     def _():
-                        self.to_dn(above).start()
-
-                    self.to_sib(above, x).start()
-
-                @pl.loop(0, 2)
-                def _(side):
-                    p = z + (2 * side - 1) * (d - 1)
-
-                    @pl.when((d > 0) & (p >= 0) & (p < Z) & (d + 1 - side > 1))
-                    def _():
+                        p = pick(arrival, k)
                         self.await_block(place(p, 1 - x, c))
                         self.to_sib(p, 1 - x).start()
-                        self.await_block(place(p, x, 1 - c))
-                        self.await_block(place(p, 1 - x, 1 - c))
-
-                        @pl.when(p == pick(arrival, Z - 1))
-                        def _():
-                            before_last()
-
-                        compute(p)
+
+                group = pick(groups, g)
+                for p in (2 * group, 2 * group + 1):
+                    for px in range(2):
+                        self.await_block(place(p, px, 1 - c))
+
+                @pl.when(g == Z // 2 - 1)
+                def _():
+                    before_last()
+
+                compute(group)
+
+        def pass_on(self, p):
+            self.await_block(place(p, x, c))
+
+            @pl.when((p < z) & has_up)
+            def _():
+                self.to_up(p).start()
+
+            @pl.when((p > z) & has_dn)
+            def _():
+                self.to_dn(p).start()
+
+            self.to_sib(p, x).start()
 
         def drain(self):
+            toward = 1 - 2 * (z % 2)
             for p in range(Z):
-                self.to_x(p).wait_send()
+                mirror = 2 * z - p
+
+                @pl.when(((p - z) * toward <= 0) | (mirror < 0) | (mirror >= Z))
+                def _():
+                    self.to_x(p).wait_send()
+
                 self.to_sib(p, 0).wait_send()
                 self.to_sib(p, 1).wait_send()
 
@@ -300,28 +323,22 @@
         def to_dn(self, p, h):
             return self.copy(self.z_send, self.dn_recv, 3, p, h, place(z - 1, x, c))
 
-        def project(self, p, acts, weight):
-            blocks = [acts[i * rows : (i + 1) * rows] for i in range(4)]
+        def project(self, group, acts, weight):
+            blocks = [acts[i * rows : (i + 1) * rows] for i in range(8)]
             first = c == 0
-            lhs = jnp.concatenate(
-                [
-                    jnp.where(first, blocks[1], blocks[0]),
-                    jnp.where(first, blocks[3], blocks[2]),
-                    jnp.where(first, blocks[0], blocks[1]),
-                    jnp.where(first, blocks[2], blocks[3]),
-                ],
-                axis=0,
-            ).astype(bf16)
-
-            @pl.loop(0, D // wide)
-            def _(k):
-                cols = pl.ds(pl.multiple_of(k * wide, wide), wide)
+            others = [jnp.where(first, blocks[i + 1], blocks[i]) for i in range(0, 8, 2)]
+            own = [jnp.where(first, blocks[i], blocks[i + 1]) for i in range(0, 8, 2)]
+            lhs = jnp.concatenate(others + own, axis=0).astype(bf16)
+            for k in range(D // wide):
+                cols = slice(k * wide, (k + 1) * wide)
                 term = jnp.dot(lhs, weight[:, cols], preferred_element_type=f32)
-                for i in range(2):
-                    self.sib_send[p, i, :, cols] = term[i * rows : (i + 1) * rows].astype(bf16)
-                    own_part[p, i, :, cols] = term[(2 + i) * rows : (3 + i) * rows]
-
-            self.to_sib(p).start()
+                for i in range(4):
+                    p = 2 * group + i // 2
+                    self.sib_send[p, i % 2, :, cols] = term[i * rows : (i + 1) * rows].astype(bf16)
+                    own_part[p, i % 2, :, cols] = term[(4 + i) * rows : (5 + i) * rows]
+
+            self.to_sib(2 * group).start()
+            self.to_sib(2 * group + 1).start()
 
         def start_x(self, j):
             p, h = pick(leaving, j // halves), j % halves
@@ -342,16 +359,18 @@
                 self.start_x(j)
 
         def run(self):
+            for j in range(halves, 2 * halves):
+                self.start_x(j)
+
             @pl.loop(0, Z * halves)
             def _(j):
-                p, h = pick(leaving, j // halves), j % halves
+                @pl.when(j + 2 * halves < Z * halves)
+                def _():
+                    self.to_x(pick(leaving, j // halves + 1), j % halves).wait_send()
+                    self.start_x(j + 2 * halves)
+
+                p, h = pick(passing, j // halves), j % halves
                 cols = pl.ds(pl.multiple_of(h * half, half), half)
-                self.to_x(p, h).wait_send()
-
-                @pl.when(j + halves < Z * halves)
-                def _():
-                    self.start_x(j + halves)
-
                 self.to_x(p, h).wait_recv()
                 kept[p, :, cols] += self.x_recv[p, :, cols].astype(f32)
 
@@ -383,6 +402,10 @@
             for p in range(Z):
                 self.to_sib(p).wait_send()
                 for h in range(halves):
+
+                    @pl.when((p == pick(leaving, 0)) | (p == pick(leaving, Z - 1)))
+                    def _():
+                        self.to_x(p, h).wait_send()
 
                     @pl.when(p > z)
                     def _():
@@ -401,40 +424,29 @@
         sib_send2, sib_recv2, x_send2, x_recv2, z_send2, up_recv2, dn_recv2, r_send2, r_recv2
     )
 
-    def lhs_of(buf, p, k):
-        return buf[pl.ds(pl.multiple_of(p * plane, plane), plane), part_of(k)]
-
-    def part_of(k):
-        return pl.ds(pl.multiple_of(k * wide, wide), wide)
-
-    def encode(p):
-        @pl.when(p == z)
+    def rows_of(buf, group):
+        return buf[pl.ds(pl.multiple_of(group * 2 * plane, 2 * plane), 2 * plane), :]
+
+    def encode(group):
+        @pl.when(group == z // 2)
         def _():
             weights[0].wait()
             weights[1].wait()
             for copy in weights[2:]:
                 copy.start()
 
-        def step(k, total):
-            return total + jnp.dot(lhs_of(gath1, p, k), enc_w[part_of(k), :], preferred_element_type=f32)
-
-        total = lax.fori_loop(0, D // wide, step, jnp.zeros((plane, enc_w.shape[1]), f32))
+        total = jnp.dot(rows_of(gath1, group), enc_w[...], preferred_element_type=f32)
         preact = total + bias_ref[...].reshape(1, -1)
         acts = preact * jax.nn.sigmoid(sharpness * (preact - thr_ref[...].reshape(1, -1)))
-        scatter1.project(p, acts, dec_w)
-
-    def feed_hidden(p):
-        def step(k, totals):
-            lhs = lhs_of(gath2, p, k)
-            return tuple(
-                total
-                + lax.dot_general(lhs, mat[:, part_of(k)], (((1,), (1,)), ((), ())), preferred_element_type=f32)
-                for total, mat in zip(totals, (gate_w, up_w))
-            )
-
-        zeros = jnp.zeros((plane, gate_w.shape[0]), f32)
-        gate_proj, up_proj = lax.fori_loop(0, D // wide, step, (zeros, zeros))
-        scatter2.project(p, jax.nn.gelu(gate_proj, approximate=True) * up_proj, down_w)
+        scatter1.project(group, acts, dec_w)
+
+    def feed_hidden(group):
+        lhs = rows_of(gath2, group)
+        gate_proj, up_proj = (
+            lax.dot_general(lhs, mat[...], (((1,), (1,)), ((), ())), preferred_element_type=f32)
+            for mat in (gate_w, up_w)
+        )
+        scatter2.project(group, jax.nn.gelu(gate_proj, approximate=True) * up_proj, down_w)
 
     block(gath1, me)[...] = res_ref[...]
     gather1.run(encode, scatter1.start_first)
@@ -532,7 +544,7 @@
 
     def per_device(residual, *rest):
         rows, width = residual.shape
-        if n % 4 == 0 and rows % 16 == 0 and width % 128 == 0:
+        if n % 8 == 0 and n > 8 and rows % 16 == 0 and width % 128 == 0:
             return fused_device(n, residual, *rest)
         return plain_device(residual, *rest)
 

time: 104 us -> 87.4 us (0.84)
  Pallas kernels: 103 us -> 85.4 us
    pallas_call x1, Pallas kernels: 103 us -> 85.4 us  [fused_device(): pl.pallas_call(functools.partial(kernel, Z, rows), out_shape=jax.ShapeDty...]
where the time goes in v3:
time: 87.4 us; the launch traced here: 87 us
  Pallas kernels  85.4 us (98%)
  local copies, waits for them, and re-layouts  1.58 us (2%)
    pallas_call x1, Pallas kernels, fused_device(): pl.pallas_call(functools.partial(kernel, Z, rows), out_shape=jax.ShapeDty...  85.4 us

profile of v3, /device:TPU:0, one launch (start us, length us, event | category | flops | bytes accessed | tf_op | source)
XLA Modules:
  0.0 87.0 jit_solution(10848482701854563968)
XLA Ops:
  0.0 85.4 %shard_map.109 = bf16[16,4608]{1,0:T(8,128)(2,1)} custom-call(bf16[16,4608]{1,0:T(8,128)(2,1)} %res_ref.1, bf16[4608,512]{1,0:T(8,128)(2,1)} %enc_hbm.1, f32[512]{0:T(512)} %bias_ref.1, f32[512]{0:T(512)} %thr_ref.1, bf16[512,4608]{1,0:T(8,128)(2,1)} %dec_hbm.1, f32[4608]{0:T(1024)} %dec_bias_ref.1, f32[4608]{0:T(1024)} %pre_gain_ref.1, ...), custom_call_target="tpu_custom_call" | custom-call | flops 3435134976 | bytes 13418496 | tf_op jit(solution)/shard_map/pallas_call | solution.py:491
  85.4 1.6 %copy.13 = bf16[16,4608]{1,0:T(8,128)(2,1)} copy(bf16[16,4608]{1,0:T(8,128)(2,1)} %shard_map.109) | data formatting | bytes 294912

commit v4 on v3

--- a/solution.py
+++ b/solution.py
@@ -231,14 +231,20 @@
                     self.pass_on(first)
                     self.to_x(first).start()
 
-                @pl.when((second >= 0) & (second < Z))
+                second_is = (second >= 0) & (second < Z)
+
+                @pl.when(second_is)
                 def _():
                     self.pass_on(second)
 
-                    @pl.when(first_is)
+                if d > 1:
+
+                    @pl.when((first - toward >= 0) & (first - toward < Z) & (second + toward >= 0) & (second + toward < Z))
                     def _():
-                        self.to_x(first).wait_send()
-
+                        self.to_x(second + toward).start()
+
+                @pl.when(second_is & jnp.logical_not(first_is))
+                def _():
                     self.to_x(second).start()
 
             @pl.loop(0, Z // 2)
@@ -276,14 +282,8 @@
             self.to_sib(p, x).start()
 
         def drain(self):
-            toward = 1 - 2 * (z % 2)
             for p in range(Z):
-                mirror = 2 * z - p
-
-                @pl.when(((p - z) * toward <= 0) | (mirror < 0) | (mirror >= Z))
-                def _():
-                    self.to_x(p).wait_send()
-
+                self.to_x(p).wait_send()
                 self.to_sib(p, 0).wait_send()
                 self.to_sib(p, 1).wait_send()
 

time: 87.4 us -> 87.3 us (level)
  no operation moved by 1% of the time
where the time goes in v4:
time: 87.3 us; the launch traced here: 86.8 us
  Pallas kernels  85.2 us (98%)
  local copies, waits for them, and re-layouts  1.58 us (2%)
    pallas_call x1, Pallas kernels, fused_device(): pl.pallas_call(functools.partial(kernel, Z, rows), out_shape=jax.ShapeDty...  85.2 us

profile of v4, /device:TPU:0, one launch (start us, length us, event | category | flops | bytes accessed | tf_op | source)
XLA Modules:
  0.0 86.8 jit_solution(7270118025774268465)
XLA Ops:
  0.0 85.2 %shard_map.109 = bf16[16,4608]{1,0:T(8,128)(2,1)} custom-call(bf16[16,4608]{1,0:T(8,128)(2,1)} %res_ref.1, bf16[4608,512]{1,0:T(8,128)(2,1)} %enc_hbm.1, f32[512]{0:T(512)} %bias_ref.1, f32[512]{0:T(512)} %thr_ref.1, bf16[512,4608]{1,0:T(8,128)(2,1)} %dec_hbm.1, f32[4608]{0:T(1024)} %dec_bias_ref.1, f32[4608]{0:T(1024)} %pre_gain_ref.1, ...), custom_call_target="tpu_custom_call" | custom-call | flops 3435134976 | bytes 13418496 | tf_op jit(solution)/shard_map/pallas_call | solution.py:491
  85.2 1.6 %copy.13 = bf16[16,4608]{1,0:T(8,128)(2,1)} copy(bf16[16,4608]{1,0:T(8,128)(2,1)} %shard_map.109) | data formatting | bytes 294912

commit v5 on v4

--- a/solution.py
+++ b/solution.py
@@ -359,16 +359,12 @@
                 self.start_x(j)
 
         def run(self):
-            for j in range(halves, 2 * halves):
+            @pl.loop(halves, Z * halves)
+            def _(j):
                 self.start_x(j)
 
             @pl.loop(0, Z * halves)
             def _(j):
-                @pl.when(j + 2 * halves < Z * halves)
-                def _():
-                    self.to_x(pick(leaving, j // halves + 1), j % halves).wait_send()
-                    self.start_x(j + 2 * halves)
-
                 p, h = pick(passing, j // halves), j % halves
                 cols = pl.ds(pl.multiple_of(h * half, half), half)
                 self.to_x(p, h).wait_recv()
@@ -402,10 +398,7 @@
             for p in range(Z):
                 self.to_sib(p).wait_send()
                 for h in range(halves):
-
-                    @pl.when((p == pick(leaving, 0)) | (p == pick(leaving, Z - 1)))
-                    def _():
-                        self.to_x(p, h).wait_send()
+                    self.to_x(p, h).wait_send()
 
                     @pl.when(p > z)
                     def _():

time: 87.3 us -> 87.2 us (level)
  no operation moved by 1% of the time
where the time goes in v5:
time: 87.2 us; the launch traced here: 86.8 us
  Pallas kernels  85.2 us (98%)
  local copies, waits for them, and re-layouts  1.58 us (2%)
    pallas_call x1, Pallas kernels, fused_device(): pl.pallas_call(functools.partial(kernel, Z, rows), out_shape=jax.ShapeDty...  85.2 us

profile of v5, /device:TPU:0, one launch (start us, length us, event | category | flops | bytes accessed | tf_op | source)
XLA Modules:
  0.0 86.8 jit_solution(2417761134228031868)
XLA Ops:
  0.0 85.2 %shard_map.109 = bf16[16,4608]{1,0:T(8,128)(2,1)} custom-call(bf16[16,4608]{1,0:T(8,128)(2,1)} %res_ref.1, bf16[4608,512]{1,0:T(8,128)(2,1)} %enc_hbm.1, f32[512]{0:T(512)} %bias_ref.1, f32[512]{0:T(512)} %thr_ref.1, bf16[512,4608]{1,0:T(8,128)(2,1)} %dec_hbm.1, f32[4608]{0:T(1024)} %dec_bias_ref.1, f32[4608]{0:T(1024)} %pre_gain_ref.1, ...), custom_call_target="tpu_custom_call" | custom-call | flops 3435134976 | bytes 13418496 | tf_op jit(solution)/shard_map/pallas_call | solution.py:484
  85.2 1.6 %copy.13 = bf16[16,4608]{1,0:T(8,128)(2,1)} copy(bf16[16,4608]{1,0:T(8,128)(2,1)} %shard_map.109) | data formatting | bytes 294912
